TPU v7x, 32 devices: a whole 2x2x4 slice. The times are simulated.
32 devices in a mesh: groups: 2 (over y), seq: 4 (over z), head: 2 (over x), pair: 2 (over core).
Axes of the slice: x: 2, y: 2, z: 4, core: 2. Of those that a mesh axis runs over, the one named last changes fastest.
Arguments:
- query_rows: bfloat16 [2048, 1024], P(('groups', 'seq'), ('head', 'pair')), parts along dimension 0, may hold values from -6 to 6
- key_rows: bfloat16 [2048, 1024], P(('groups', 'seq'), ('head', 'pair')), parts along dimension 0, may hold values from -6 to 6
- value_rows: bfloat16 [2048, 1024], P(('groups', 'seq'), ('head', 'pair')), parts along dimension 0, may hold values from -6 to 6
- out_grad: bfloat16 [2048, 1024], P(('groups', 'seq'), ('head', 'pair')), parts along dimension 0, may hold values from -6 to 6
- random_blocks: int32 [32, 16, 3], P(('groups', 'head', 'pair'), 'seq'), parts along dimension 0, may hold values from 0 to 15, as said below
- global_positions: int32 [256], P('groups'), parts along dimension 0, may hold values from 0 to 1023, as said below
Outputs:
- attended: bfloat16 [2048, 1024], P(('groups', 'seq'), ('head', 'pair')), parts along dimension 0
- grad_query: bfloat16 [2048, 1024], P(('groups', 'seq'), ('head', 'pair')), parts along dimension 0
- grad_key: bfloat16 [2048, 1024], P(('groups', 'seq'), ('head', 'pair')), parts along dimension 0
- grad_value: bfloat16 [2048, 1024], P(('groups', 'seq'), ('head', 'pair')), parts along dimension 0
There are 2 independent parts, one for each index of `groups`. A program takes and returns all parts, laid end to end along the dimension named above; each array names one. Nothing has to cross between parts.
Inputs may be any that keep to these rules, and one draw needn't show every extreme that they name: `random_blocks`: A query block's 3 random blocks are distinct, lie on another index of seq than the block itself (indices of seq hold 4 blocks each) and never in its window. For each head, the random blocks of the 4 query blocks of one index of seq take at most 4 blocks from any one index of seq, and this most is reached. `global_positions`: 128 distinct positions in increasing order.
All inputs are finite; a program needn't handle non-finite values.
Results may differ from a plain program's by a relative error of at most 0.0096.
The roundings to bfloat16 on the way count: a program that leaves them out, or rounds other values in their place, can miss the bound.
Values may be sent and summed in bfloat16 or wider, within the bound.
A program may use at most 64 MiB of HBM per device.

v0:
```python
from functools import partial
import math

import jax
import jax.numpy as jnp
from jax import lax
from jax.experimental import pallas as pl
from jax.experimental.pallas import tpu as pltpu
from jax.sharding import PartitionSpec as P

HD = 64
BLK = 64
RAND = 3


def padded_2(array, sides, width):
    for axis, dim in sides:
        peers, length = (lax.axis_size(axis), array.shape[dim])
        up = [(i, (i + 1) % peers) for i in range(peers - 1)]
        down = [(j, i) for i, j in up]
        last = lax.slice_in_dim(array, length - width, length, axis=dim)
        leading = lax.slice_in_dim(array, 0, width, axis=dim)
        before = lax.ppermute(last, axis, up)
        after = lax.ppermute(leading, axis, down)
        array = jnp.concatenate([before, array, after], axis=dim)
    return array


def from_behind(array, axis, by):
    peers = lax.axis_size(axis)
    pairs = [(i, i + by) for i in range(peers) if 0 <= i + by < peers]
    return lax.ppermute(array, axis, pairs)


def softmax_rows(scores):
    top = jnp.max(scores, axis=-1, keepdims=True)
    raised = jnp.exp(scores - top)
    return raised / jnp.sum(raised, axis=-1, keepdims=True)


def group_probs(query, window, far_rows, global_rows, window_valid, global_keep, scale):
    near = (
        jnp.einsum("bihd,bjhd->bhij", query, window[..., :HD], preferred_element_type=jnp.float32)
        * scale
    )
    far = (
        jnp.einsum("bihd,bjhd->bhij", query, far_rows[..., :HD], preferred_element_type=jnp.float32)
        * scale
    )
    wide = (
        jnp.einsum(
            "bihd,jhd->bhij", query, global_rows[..., :HD], preferred_element_type=jnp.float32
        )
        * scale
    )
    near = jnp.where(window_valid[:, None, None, :], near, -jnp.inf)
    wide = jnp.where(global_keep[:, :, None, :], wide, -jnp.inf)
    return softmax_rows(jnp.concatenate([near, far, wide], axis=-1))


def split_keys(values, window, far_rows):
    span = window.shape[1]
    reach = far_rows.shape[1]
    return (values[..., :span], values[..., span : span + reach], values[..., span + reach :])


def forward_group(items, global_rows, scale):
    query, window, far_rows, window_valid, global_keep = items
    weights = group_probs(
        query, window, far_rows, global_rows, window_valid, global_keep, scale
    ).astype(jnp.bfloat16)
    near, far, wide = split_keys(weights, window, far_rows)
    out = jnp.einsum("bhij,bjhd->bihd", near, window[..., HD:], preferred_element_type=jnp.float32)
    out = out + jnp.einsum(
        "bhij,bjhd->bihd", far, far_rows[..., HD:], preferred_element_type=jnp.float32
    )
    return out + jnp.einsum(
        "bhij,jhd->bihd", wide, global_rows[..., HD:], preferred_element_type=jnp.float32
    )


def backward_group(items, global_rows, scale):
    query, window, far_rows, window_valid, global_keep, grad_out, delta = items
    probs = group_probs(query, window, far_rows, global_rows, window_valid, global_keep, scale)
    weights = probs.astype(jnp.bfloat16)
    value_dot = jnp.concatenate(
        [
            jnp.einsum(
                "bihd,bjhd->bhij", grad_out, window[..., HD:], preferred_element_type=jnp.float32
            ),
            jnp.einsum(
                "bihd,bjhd->bhij", grad_out, far_rows[..., HD:], preferred_element_type=jnp.float32
            ),
            jnp.einsum(
                "bihd,jhd->bhij",
                grad_out,
                global_rows[..., HD:],
                preferred_element_type=jnp.float32,
            ),
        ],
        axis=-1,
    )
    dscore = (probs * (value_dot - jnp.transpose(delta, (0, 2, 1))[..., None])).astype(jnp.bfloat16)
    dnear, dfar, dwide = split_keys(dscore, window, far_rows)
    near, far, wide = split_keys(weights, window, far_rows)
    grad_query = jnp.einsum(
        "bhij,bjhd->bihd", dnear, window[..., :HD], preferred_element_type=jnp.float32
    )
    grad_query = grad_query + jnp.einsum(
        "bhij,bjhd->bihd", dfar, far_rows[..., :HD], preferred_element_type=jnp.float32
    )
    grad_query = scale * (
        grad_query
        + jnp.einsum(
            "bhij,jhd->bihd", dwide, global_rows[..., :HD], preferred_element_type=jnp.float32
        )
    )
    grad_window = jnp.concatenate(
        [
            scale * jnp.einsum("bhij,bihd->bjhd", dnear, query, preferred_element_type=jnp.float32),
            jnp.einsum("bhij,bihd->bjhd", near, grad_out, preferred_element_type=jnp.float32),
        ],
        axis=-1,
    )
    grad_far = jnp.concatenate(
        [
            scale * jnp.einsum("bhij,bihd->bjhd", dfar, query, preferred_element_type=jnp.float32),
            jnp.einsum("bhij,bihd->bjhd", far, grad_out, preferred_element_type=jnp.float32),
        ],
        axis=-1,
    ).astype(jnp.bfloat16)
    grad_wide = jnp.concatenate(
        [
            scale * jnp.einsum("bhij,bihd->jhd", dwide, query, preferred_element_type=jnp.float32),
            jnp.einsum("bhij,bihd->jhd", wide, grad_out, preferred_element_type=jnp.float32),
        ],
        axis=-1,
    )
    return (grad_query, grad_window, grad_far, grad_wide)


def local_wide(query_rows, key_rows, value_rows, out_grad, random_blocks, global_positions):
    tokens = query_rows.shape[0]
    heads = query_rows.shape[1] // HD
    blocks = tokens // BLK
    devices = lax.axis_size("seq")
    place = lax.axis_index("seq")
    scale = 1.0 / math.sqrt(HD)
    capacity = RAND * (blocks // (devices - 1)) + min(RAND, blocks % (devices - 1))
    group = math.gcd(blocks, max(1, 512 // BLK))
    count = blocks // group
    local_index = global_positions - place * tokens
    owned = (local_index >= 0) & (local_index < tokens)
    target = jnp.where(owned, local_index, tokens)
    safe_index = jnp.where(owned, local_index, 0)

    def pick(rows):
        return jnp.where(owned[:, None], rows[safe_index].astype(jnp.float32), 0.0)

    glob_sum = (
        lax.psum(pick(query_rows).astype(jnp.bfloat16), "seq").astype(jnp.float32),
        lax.psum(pick(key_rows).astype(jnp.bfloat16), "seq").astype(jnp.float32),
        lax.psum(pick(value_rows).astype(jnp.bfloat16), "seq").astype(jnp.float32),
        lax.psum(pick(out_grad).astype(jnp.bfloat16), "seq").astype(jnp.float32),
    )
    glob_query = glob_sum[0].astype(jnp.bfloat16).reshape(-1, heads, HD)
    glob_key = glob_sum[1].astype(jnp.bfloat16).reshape(-1, heads, HD)
    glob_value = glob_sum[2].astype(jnp.bfloat16).reshape(-1, heads, HD)
    glob_grad = glob_sum[3].astype(jnp.bfloat16).reshape(-1, heads, HD)
    global_rows = jnp.concatenate([glob_key, glob_value], axis=-1)
    query3 = query_rows.reshape(tokens, heads, HD)
    key3 = key_rows.reshape(tokens, heads, HD)
    value3 = value_rows.reshape(tokens, heads, HD)
    pair_rows = jnp.concatenate([key3, value3], axis=-1)
    padded = padded_2(pair_rows, (("seq", 0),), BLK)
    framed = padded.reshape(blocks + 2, BLK, heads, 2 * HD)
    window = jnp.concatenate([framed[:-2], framed[1:-1], framed[2:]], axis=1)
    block_ids = place * blocks + jnp.arange(blocks)
    neighbour = block_ids[:, None] + (jnp.repeat(jnp.arange(3), BLK) - 1)[None, :]
    window_valid = (neighbour >= 0) & (neighbour < devices * blocks)
    global_block = global_positions // BLK
    near_glob = jnp.abs(global_block[None, :] - block_ids[:, None]) <= 1
    in_random = jnp.any(random_blocks[:, :, :, None] == global_block[None, None, None, :], axis=2)
    global_keep = jnp.logical_not(near_glob[:, None, :] | jnp.transpose(in_random, (1, 0, 2)))
    owner = random_blocks // blocks
    local_block = random_blocks % blocks
    flat_owner = owner.reshape(heads, blocks * RAND)
    hits = (flat_owner[:, :, None] == jnp.arange(devices)[None, None, :]).astype(jnp.int32)
    before = jnp.cumsum(hits, axis=1) - hits
    flat_slot = jnp.sum(before * hits, axis=2)
    placed = (flat_slot[:, :, None] == jnp.arange(capacity)[None, None, :]).astype(jnp.int32)
    marks = (local_block.reshape(heads, blocks * RAND) + 1)[:, :, None, None]
    table = jnp.sum(hits[:, :, :, None] * placed[:, :, None, :] * marks, axis=1) - 1
    asked = lax.all_to_all(
        jnp.transpose(table, (1, 0, 2)), "seq", split_axis=0, concat_axis=0, tiled=True
    )
    own_blocks = pair_rows.reshape(blocks, BLK, heads, 2 * HD)
    wanted = (jnp.maximum(asked, 0)[..., None] == jnp.arange(blocks)).astype(jnp.bfloat16)
    served = jnp.einsum(
        "zhcb,bthf->zhctf", wanted, own_blocks, preferred_element_type=jnp.float32
    ).astype(jnp.bfloat16)
    owner_order = jnp.transpose(owner, (1, 2, 0))
    slot_order = jnp.transpose(flat_slot.reshape(heads, blocks, RAND), (1, 2, 0))
    head_order = jnp.arange(heads)[None, None, :]
    arrived = lax.all_to_all(served, "seq", split_axis=0, concat_axis=0, tiled=True)
    arrived = jnp.transpose(arrived, (0, 2, 1, 3, 4)).reshape(
        devices * capacity, heads, BLK, 2 * HD
    )
    source = owner_order * capacity + slot_order
    chosen = (source[..., None] == jnp.arange(devices * capacity)).astype(jnp.bfloat16)
    picked = jnp.einsum(
        "brhz,zhtf->brhtf", chosen, arrived, preferred_element_type=jnp.float32
    ).astype(jnp.bfloat16)
    far_rows = jnp.transpose(picked, (0, 1, 3, 2, 4)).reshape(blocks, RAND * BLK, heads, 2 * HD)

    def grouped(array):
        return array.reshape((count, group) + array.shape[1:])

    query_blocks = query3.reshape(blocks, BLK, heads, HD)
    sparse_out = lax.map(
        partial(forward_group, global_rows=global_rows, scale=scale),
        (
            grouped(query_blocks),
            grouped(window),
            grouped(far_rows),
            grouped(window_valid),
            grouped(global_keep),
        ),
    )
    sparse_out = sparse_out.reshape(tokens, heads, HD)
    wide = jnp.einsum("ghd,thd->hgt", glob_query, key3, preferred_element_type=jnp.float32) * scale
    local_top = jnp.max(wide, axis=-1)
    top = lax.pmax(local_top, "seq")
    total = lax.psum(jnp.sum(jnp.exp(wide - top[..., None]), axis=-1), "seq")
    glob_probs = jnp.exp(wide - top[..., None]) / total[..., None]
    glob_weights = glob_probs.astype(jnp.bfloat16)
    glob_part = jnp.einsum("hgt,thd->ghd", glob_weights, value3, preferred_element_type=jnp.float32)
    glob_out = lax.psum(glob_part, "seq").astype(jnp.bfloat16)
    attended = sparse_out.astype(jnp.bfloat16).at[target].set(glob_out, mode="drop")
    glob_mask = jnp.zeros((tokens,), jnp.bool_).at[target].set(True, mode="drop")
    sparse_grad = jnp.where(
        glob_mask[:, None, None],
        jnp.zeros_like(out_grad.reshape(tokens, heads, HD)),
        out_grad.reshape(tokens, heads, HD),
    )
    delta = jnp.sum(sparse_grad.astype(jnp.float32) * attended.astype(jnp.float32), axis=-1)
    grad_query, grad_window, grad_far, grad_wide = lax.map(
        partial(backward_group, global_rows=global_rows, scale=scale),
        (
            grouped(query_blocks),
            grouped(window),
            grouped(far_rows),
            grouped(window_valid),
            grouped(global_keep),
            grouped(sparse_grad.reshape(blocks, BLK, heads, HD)),
            grouped(delta.reshape(blocks, BLK, heads)),
        ),
    )
    grad_query = grad_query.reshape(tokens, heads, HD)
    grad_window = grad_window.reshape(blocks, 3, BLK, heads, 2 * HD)
    grad_wide = jnp.sum(grad_wide, axis=0)
    folded = jnp.zeros((blocks + 2, BLK, heads, 2 * HD), jnp.float32)
    folded = (
        folded.at[0:blocks]
        .add(grad_window[:, 0])
        .at[1 : blocks + 1]
        .add(grad_window[:, 1])
        .at[2 : blocks + 2]
        .add(grad_window[:, 2])
    )
    from_right = from_behind(folded[0], "seq", -1)
    from_left = from_behind(folded[blocks + 1], "seq", 1)
    local_pair = folded[1 : blocks + 1]
    local_pair = local_pair.at[blocks - 1].add(from_right).at[0].add(from_left)
    far_terms = jnp.transpose(grad_far.reshape(blocks, RAND, BLK, heads, 2 * HD), (0, 1, 3, 2, 4))
    outgoing = (
        jnp.zeros((devices, heads, capacity, BLK, 2 * HD), jnp.bfloat16)
        .at[owner_order, head_order, slot_order]
        .set(far_terms)
    )
    returned = lax.all_to_all(outgoing, "seq", split_axis=0, concat_axis=0, tiled=True)
    landing = jnp.where(asked >= 0, asked, blocks)
    gathered = (
        jnp.zeros((blocks, heads, BLK, 2 * HD), jnp.float32)
        .at[landing, jnp.arange(heads)[None, :, None]]
        .add(returned.astype(jnp.float32), mode="drop")
    )
    pair_grad = local_pair.reshape(tokens, heads, 2 * HD) + jnp.transpose(
        gathered, (0, 2, 1, 3)
    ).reshape(tokens, heads, 2 * HD)
    glob_attended = glob_out.astype(jnp.float32)
    glob_delta = jnp.sum(glob_grad.astype(jnp.float32) * glob_attended, axis=-1)
    glob_dot = jnp.einsum("ghd,thd->hgt", glob_grad, value3, preferred_element_type=jnp.float32)
    glob_dscore = (glob_probs * (glob_dot - jnp.transpose(glob_delta)[..., None])).astype(
        jnp.bfloat16
    )
    query_part = scale * jnp.einsum(
        "hgt,thd->ghd", glob_dscore, key3, preferred_element_type=jnp.float32
    )
    key_from_glob = scale * jnp.einsum(
        "hgt,ghd->thd", glob_dscore, glob_query, preferred_element_type=jnp.float32
    )
    value_from_glob = jnp.einsum(
        "hgt,ghd->thd", glob_weights, glob_grad, preferred_element_type=jnp.float32
    )
    summed = lax.psum((query_part, grad_wide), "seq")
    grad_query = grad_query.at[target].add(summed[0], mode="drop")
    pair_grad = pair_grad.at[target].add(summed[1], mode="drop")
    grad_key = pair_grad[..., :HD] + key_from_glob
    grad_value = pair_grad[..., HD:] + value_from_glob
    return (
        attended.reshape(tokens, heads * HD),
        grad_query.reshape(tokens, heads * HD).astype(jnp.bfloat16),
        grad_key.reshape(tokens, heads * HD).astype(jnp.bfloat16),
        grad_value.reshape(tokens, heads * HD).astype(jnp.bfloat16),
    )


BIG = 1e30
LIMIT = 63 * 1024 * 1024
NT = (((1,), (1,)), ((), ()))
TN = (((0,), (0,)), ((), ()))
NN = (((1,), (0,)), ((), ()))


def mm(left, right, dims):
    return lax.dot_general(left, right, dims, preferred_element_type=jnp.float32)


def head_kernel(
    n, tokens, q_hbm, k_hbm, v_hbm, g_hbm, rb_hbm, gp_hbm, att_hbm, dq_hbm, dk_hbm, dv_hbm,
    att_ref, dq_ref, dk_ref, dv_ref, q_ref, k_ref, v_ref, g_ref, rb_ref, gp_ref, kq_send, vd_send, tab_send, kq, vd, tab, o1_send, o2_send, o1, o2,
    ka, qa, probs, weights, dscore, load_sem, store_sem, send_sem, recv_sem,
):
    me = lax.axis_index("seq")
    total = n * tokens
    qb = tokens // BLK
    scale = 1.0 / math.sqrt(HD)
    peers = [lax.rem(me + off, n) for off in range(1, n)]
    sources = [lax.rem(me + n - off, n) for off in range(1, n)]

    loads = [
        pltpu.make_async_copy(hbm, vmem, load_sem.at[i])
        for i, (hbm, vmem) in enumerate(
            ((k_hbm, k_ref), (q_hbm, q_ref), (v_hbm, v_ref), (g_hbm, g_ref), (rb_hbm, rb_ref), (gp_hbm, gp_ref))
        )
    ]
    for load in loads:
        load.start()
    barrier = pltpu.get_barrier_semaphore()
    for peer in peers:
        pl.semaphore_signal(
            barrier, inc=1, device_id={"seq": peer}, device_id_type=pl.DeviceIdType.MESH
        )

    def copy(stage, off, send, recv, slot):
        return pltpu.make_async_remote_copy(
            src_ref=send.at[peers[off - 1]],
            dst_ref=recv.at[slot],
            send_sem=send_sem.at[stage, off - 1],
            recv_sem=recv_sem.at[stage, off - 1],
            device_id={"seq": peers[off - 1]},
            device_id_type=pl.DeviceIdType.MESH,
        )

    def start(stage, off, send, recv):
        copy(stage, off, send, recv, me).start()

    def arrive(stage, off, send, recv):
        copy(stage, off, send, recv, sources[off - 1]).wait_recv()

    row = lax.broadcasted_iota(jnp.int32, (8, 128), 0)
    lane = lax.broadcasted_iota(jnp.int32, (8, 128), 1)
    loads[4].wait()
    for h in range(n):
        mark = jnp.zeros((8, 128), jnp.float32)
        for b in range(qb):
            hit = lane == rb_ref[0, h, b]
            for r in range(1, RAND):
                hit = hit | (lane == rb_ref[r, h, b])
            mark = jnp.where(hit & (row == b), 1.0, mark)
        tab_send[h] = mark
    loads[0].wait()
    loads[1].wait()
    for h in range(n):
        cols = slice(h * HD, (h + 1) * HD)
        kq_send[h, :, 0:HD] = k_ref[:, cols]
        kq_send[h, :, HD : 2 * HD] = q_ref[:, cols] * jnp.bfloat16(scale)
    pl.semaphore_wait(barrier, n - 1)
    order = [2, 1, 3] if n == 4 else list(range(1, n))
    for off in order:
        start(0, off, tab_send, tab)
        start(1, off, kq_send, kq)
    loads[2].wait()
    loads[3].wait()
    for h in range(n):
        cols = slice(h * HD, (h + 1) * HD)
        vd_send[h, :, 0:HD] = v_ref[:, cols]
        vd_send[h, :, HD : 2 * HD] = g_ref[:, cols]
    for off in order:
        start(2, off, vd_send, vd)
    kq[me] = kq_send[me]
    vd[me] = vd_send[me]
    tab[me] = tab_send[me]

    pos = lax.broadcasted_iota(jnp.int32, (total, 128), 0)
    col = lax.broadcasted_iota(jnp.int32, (total, 128), 1)
    loads[5].wait()
    globals_here = gp_ref.shape[1]
    spots = lax.broadcasted_iota(jnp.int32, (total, globals_here), 0) == gp_ref[...]
    spread = mm(
        jnp.where(spots, 1.0, 0.0).astype(jnp.bfloat16),
        jnp.ones((globals_here, 128), jnp.bfloat16),
        NN,
    )
    is_global = spread > 0.5
    slot = col - HD
    block = (slot // 8) * qb + slot % 8
    mine = (slot >= 0) & (slot < 8 * n) & (slot % 8 < qb)
    key_block = pos // BLK
    near = mine & (block - key_block <= 1) & (key_block - block <= 1)
    open_key = near | is_global
    hot = jnp.where(mine & (block == key_block) & jnp.logical_not(is_global), 1.0, 0.0)
    place = jnp.where(col == key_block, 1.0, 0.0).astype(jnp.bfloat16)

    for off in order:
        arrive(0, off, tab_send, tab)
        arrive(1, off, kq_send, kq)
    table = jnp.concatenate(
        [
            jnp.zeros((HD, 128), jnp.float32),
            tab[...].reshape(8 * n, 128),
            jnp.zeros((128 - HD - 8 * n, 128), jnp.float32),
        ],
        axis=0,
    ).astype(jnp.bfloat16)
    chosen = mm(place, table, NT)
    bias = jnp.where(open_key | (chosen > 0.5), 0.0, -BIG).astype(jnp.bfloat16)
    pair = kq[...].reshape(total, 128)
    ka[...] = bias
    ka[:, 0:HD] = pair[:, 0:HD]
    qa[...] = hot.astype(jnp.bfloat16)
    qa[:, 0:HD] = pair[:, HD : 2 * HD]

    keys = ka[...]
    for a in range(n):
        rows = pl.ds(a * tokens, tokens)
        score = mm(keys, qa[rows, :], NT)
        top = jnp.max(score, axis=0, keepdims=True)
        raised = jnp.exp(score - top)
        prob = raised * (1.0 / jnp.sum(raised, axis=0, keepdims=True))
        probs[a] = prob
        weights[a] = prob.astype(jnp.bfloat16)

    for off in order:
        arrive(2, off, vd_send, vd)
    values = vd[...].reshape(total, 2 * HD)[:, 0:HD]
    values_t = values.T
    keys_t = keys[:, 0:HD].T
    steps = order + [0]
    deltas = []
    for off in steps:
        a = lax.rem(me + off, n)
        rows = pl.ds(pl.multiple_of(a * tokens, tokens), tokens)
        out = mm(values_t, weights[a], NN).T.astype(jnp.bfloat16)
        grad = vd[a, :, HD : 2 * HD]
        deltas.append(jnp.sum(grad.astype(jnp.float32).T * out.astype(jnp.float32).T, axis=0, keepdims=True))
        dv = jnp.zeros((tokens, HD), jnp.float32)
        for c in range(n):
            dv = dv + mm(weights[c, rows, :], vd[c, :, HD : 2 * HD], NN)
        o1_send[a, :, 0:HD] = out
        o1_send[a, :, HD : 2 * HD] = dv.astype(jnp.bfloat16)
        if off:
            start(3, off, o1_send, o1)
        else:
            o1[me] = o1_send[me]

    for step, off in enumerate(steps):
        a = lax.rem(me + off, n)
        dprob = mm(values, vd[a, :, HD : 2 * HD], NT)
        ds = (probs[a] * (dprob - deltas[step])).astype(jnp.bfloat16)
        dscore[a] = ds
        dq = mm(keys_t, ds, NN).T * scale
        o2_send[a, :, 0:HD] = dq.astype(jnp.bfloat16)
    for off in steps:
        a = lax.rem(me + off, n)
        rows = pl.ds(pl.multiple_of(a * tokens, tokens), tokens)
        dk = jnp.zeros((tokens, HD), jnp.float32)
        for c in range(n):
            dk = dk + mm(dscore[c, rows, :], qa[c * tokens : (c + 1) * tokens, 0:HD], NN)
        o2_send[a, :, HD : 2 * HD] = dk.astype(jnp.bfloat16)
        if off:
            start(4, off, o2_send, o2)
        else:
            o2[me] = o2_send[me]

    for off in order:
        arrive(3, off, o1_send, o1)
    for h in range(n):
        cols = slice(h * HD, (h + 1) * HD)
        att_ref[:, cols] = o1[h, :, 0:HD]
        dv_ref[:, cols] = o1[h, :, HD : 2 * HD]
    stores = [
        pltpu.make_async_copy(vmem, hbm, store_sem.at[i])
        for i, (vmem, hbm) in enumerate(
            ((att_ref, att_hbm), (dv_ref, dv_hbm), (dq_ref, dq_hbm), (dk_ref, dk_hbm))
        )
    ]
    stores[0].start()
    stores[1].start()
    for off in order:
        arrive(4, off, o2_send, o2)
    for h in range(n):
        cols = slice(h * HD, (h + 1) * HD)
        dq_ref[:, cols] = o2[h, :, 0:HD]
        dk_ref[:, cols] = o2[h, :, HD : 2 * HD]
    stores[2].start()
    stores[3].start()
    for stage, (send, recv) in enumerate(
        ((tab_send, tab), (kq_send, kq), (vd_send, vd), (o1_send, o1), (o2_send, o2))
    ):
        for off in order:
            copy(stage, off, send, recv, me).wait_send()
    for store in stores:
        store.wait()


def write_out(*refs):
    count = len(refs) // 3
    sources, targets, held = refs[:count], refs[count : 2 * count], refs[2 * count : 3 * count]
    sem = refs[-1]
    loads = [pltpu.make_async_copy(sources[i], held[i], sem.at[0, i]) for i in range(count)]
    stores = [pltpu.make_async_copy(held[i], targets[i], sem.at[1, i]) for i in range(count)]
    for load in loads:
        load.start()
    for load, store in zip(loads, stores):
        load.wait()
        store.start()
    for store in stores:
        store.wait()


def local_heads(query_rows, key_rows, value_rows, out_grad, random_blocks, global_positions):
    tokens, width = query_rows.shape
    n = lax.axis_size("seq")
    total = n * tokens
    bf16, f32 = jnp.bfloat16, jnp.float32
    where_it_lies = pl.BlockSpec(memory_space=pltpu.HBM)
    rows = [pltpu.VMEM((tokens, width), bf16)] * 4
    part = pltpu.VMEM((n, tokens, 2 * HD), bf16)
    small = pltpu.VMEM((n, 8, 128), f32)
    results = pl.pallas_call(
        partial(head_kernel, n, tokens),
        out_shape=[jax.ShapeDtypeStruct((tokens, width), bf16)] * 4,
        in_specs=[where_it_lies] * 6,
        out_specs=[where_it_lies] * 4,
        scratch_shapes=[
            *rows, *rows, pltpu.SMEM((RAND,) + random_blocks.shape[:2], jnp.int32), pltpu.VMEM((1, global_positions.shape[0]), jnp.int32), part, part, small, part, part, small, part, part, part, part,
            pltpu.VMEM((total, 128), bf16),
            pltpu.VMEM((total, 128), bf16),
            pltpu.VMEM((n, total, tokens), f32),
            pltpu.VMEM((n, total, tokens), bf16),
            pltpu.VMEM((n, total, tokens), bf16),
            pltpu.SemaphoreType.DMA((6,)),
            pltpu.SemaphoreType.DMA((4,)),
            pltpu.SemaphoreType.DMA((5, n - 1)),
            pltpu.SemaphoreType.DMA((5, n - 1)),
        ],
        compiler_params=pltpu.CompilerParams(
            collective_id=0, has_side_effects=True, vmem_limit_bytes=LIMIT
        ),
        cost_estimate=pl.CostEstimate(
            flops=14 * total * total * HD, bytes_accessed=16 * tokens * width, transcendentals=total * total
        ),
    )(
        query_rows, key_rows, value_rows, out_grad,
        jnp.transpose(random_blocks, (2, 0, 1)), global_positions.reshape(1, -1),
    )
    return pl.pallas_call(
        write_out,
        out_shape=[jax.ShapeDtypeStruct((tokens, width), bf16)] * 4,
        in_specs=[where_it_lies] * 4,
        out_specs=[where_it_lies] * 4,
        scratch_shapes=rows + [pltpu.SemaphoreType.DMA((2, 4))],
        compiler_params=pltpu.CompilerParams(vmem_limit_bytes=LIMIT),
    )(*results)


def local(query_rows, key_rows, value_rows, out_grad, random_blocks, global_positions):
    n = lax.axis_size("seq")
    tokens = query_rows.shape[0]
    one_head_each = query_rows.shape[1] == n * HD and n > 1
    fits = 8 * n <= 128 - HD and tokens // BLK <= 8 and n * tokens // BLK <= 128
    if one_head_each and fits and tokens % 256 == 0 and n * tokens <= 1024:
        run = local_heads
    else:
        run = local_wide
    return run(query_rows, key_rows, value_rows, out_grad, random_blocks, global_positions)


def solution(mesh):
    placed = (
        P(("groups", "seq"), ("head", "pair")),
        P(("groups", "seq"), ("head", "pair")),
        P(("groups", "seq"), ("head", "pair")),
        P(("groups", "seq"), ("head", "pair")),
        P(("groups", "head", "pair"), "seq", None),
        P("groups"),
    )
    return jax.shard_map(
        local,
        mesh=mesh,
        in_specs=placed,
        out_specs=(
            P(("groups", "seq"), ("head", "pair")),
            P(("groups", "seq"), ("head", "pair")),
            P(("groups", "seq"), ("head", "pair")),
            P(("groups", "seq"), ("head", "pair")),
        ),
        check_vma=False,
    )
```

profile of v0, /device:TPU:0, one launch (start us, length us, event | category | flops | bytes accessed | tf_op | source)
XLA Modules:
  0.0 32.9 jit_solution(17799304243538457696)
XLA Ops:
  0.6 30.4 %shard_map.93 = (bf16[256,256]{1,0:T(8,128)(2,1)}, bf16[256,256]{1,0:T(8,128)(2,1)}, bf16[256,256]{1,0:T(8,128)(2,1)}, bf16[256,256]{1,0:T(8,128)(2,1)}) custom-call(bf16[256,256]{1,0:T(8,128)(2,1)} %q_hbm.1, bf16[256,256]{1,0:T(8,128)(2,1)} %k_hbm.1, bf16[256,256]{1,0:T(8,128)(2,1)} %v_hbm.1, bf16[256,256]{1,0:T(8,128)(2,1)} %g_hbm.1, s32[3,4,4]{2,1,0:T(4,128)} %bitcast.2, ...), custom_call_target="tpu_custom_call" | custom-call | flops 939524096 | bytes 1048576 | tf_op jit(solution)/shard_map/pallas_call | solution.py:552
  31.1 1.8 %shard_map.94 = (bf16[256,256]{1,0:T(8,128)(2,1)}, bf16[256,256]{1,0:T(8,128)(2,1)}, bf16[256,256]{1,0:T(8,128)(2,1)}, bf16[256,256]{1,0:T(8,128)(2,1)}) custom-call(bf16[256,256]{1,0:T(8,128)(2,1)} %get-tuple-element.8.refs_0_, bf16[256,256]{1,0:T(8,128)(2,1)} %get-tuple-element.9.refs_1_, bf16[256,256]{1,0:T(8,128)(2,1)} %get-tuple-element.10.refs_2_, ...), custom_call_target="tpu_custom_call" | custom-call | tf_op jit(solution)/shard_map/pallas_call | solution.py:579
where the time goes:
time: 33 us; the launch traced here: 32.9 us
  Pallas kernels  32.2 us (98%)
  between operations  0.64 us (2%)
    pallas_call x1, Pallas kernels, local_heads(): pl.pallas_call(partial(head_kernel, n, tokens), out_shape=[jax.ShapeDtype...  30.4 us
    pallas_call x1, Pallas kernels, local_heads(): pl.pallas_call(write_out, out_shape=[jax.ShapeDtypeStruct((tokens, width)...  1.82 us

commit v1 on v0

--- a/solution.py
+++ b/solution.py
@@ -328,9 +328,9 @@
 
 
 def head_kernel(
-    n, tokens, q_hbm, k_hbm, v_hbm, g_hbm, rb_hbm, gp_hbm, att_hbm, dq_hbm, dk_hbm, dv_hbm,
-    att_ref, dq_ref, dk_ref, dv_ref, q_ref, k_ref, v_ref, g_ref, rb_ref, gp_ref, kq_send, vd_send, tab_send, kq, vd, tab, o1_send, o2_send, o1, o2,
-    ka, qa, probs, weights, dscore, load_sem, store_sem, send_sem, recv_sem,
+    n, tokens, q_hbm, k_hbm, v_hbm, g_hbm, rb_hbm, gp_hbm, att_ref, dq_ref, dk_ref, dv_ref,
+    q_ref, k_ref, v_ref, g_ref, rb_ref, gp_ref, kq_send, vd_send, tab_send, kq, vd, tab, o1_send, o2_send, o1, o2,
+    ka, qa, probs, weights, dscore, load_sem, send_sem, recv_sem,
 ):
     me = lax.axis_index("seq")
     total = n * tokens
@@ -500,41 +500,24 @@
         cols = slice(h * HD, (h + 1) * HD)
         att_ref[:, cols] = o1[h, :, 0:HD]
         dv_ref[:, cols] = o1[h, :, HD : 2 * HD]
-    stores = [
-        pltpu.make_async_copy(vmem, hbm, store_sem.at[i])
-        for i, (vmem, hbm) in enumerate(
-            ((att_ref, att_hbm), (dv_ref, dv_hbm), (dq_ref, dq_hbm), (dk_ref, dk_hbm))
-        )
-    ]
-    stores[0].start()
-    stores[1].start()
     for off in order:
         arrive(4, off, o2_send, o2)
     for h in range(n):
         cols = slice(h * HD, (h + 1) * HD)
         dq_ref[:, cols] = o2[h, :, 0:HD]
         dk_ref[:, cols] = o2[h, :, HD : 2 * HD]
-    stores[2].start()
-    stores[3].start()
     for stage, (send, recv) in enumerate(
         ((tab_send, tab), (kq_send, kq), (vd_send, vd), (o1_send, o1), (o2_send, o2))
     ):
         for off in order:
             copy(stage, off, send, recv, me).wait_send()
+
+
+def write_out(*refs):
+    count = len(refs) // 2
+    sources, targets, sem = refs[:count], refs[count : 2 * count], refs[-1]
+    stores = [pltpu.make_async_copy(sources[i], targets[i], sem.at[i]) for i in range(count)]
     for store in stores:
-        store.wait()
-
-
-def write_out(*refs):
-    count = len(refs) // 3
-    sources, targets, held = refs[:count], refs[count : 2 * count], refs[2 * count : 3 * count]
-    sem = refs[-1]
-    loads = [pltpu.make_async_copy(sources[i], held[i], sem.at[0, i]) for i in range(count)]
-    stores = [pltpu.make_async_copy(held[i], targets[i], sem.at[1, i]) for i in range(count)]
-    for load in loads:
-        load.start()
-    for load, store in zip(loads, stores):
-        load.wait()
         store.start()
     for store in stores:
         store.wait()
@@ -551,18 +534,17 @@
     small = pltpu.VMEM((n, 8, 128), f32)
     results = pl.pallas_call(
         partial(head_kernel, n, tokens),
-        out_shape=[jax.ShapeDtypeStruct((tokens, width), bf16)] * 4,
+        out_shape=[pltpu.VMEM((tokens, width), bf16)] * 4,
         in_specs=[where_it_lies] * 6,
-        out_specs=[where_it_lies] * 4,
+        out_specs=[pl.BlockSpec(memory_space=pltpu.VMEM)] * 4,
         scratch_shapes=[
-            *rows, *rows, pltpu.SMEM((RAND,) + random_blocks.shape[:2], jnp.int32), pltpu.VMEM((1, global_positions.shape[0]), jnp.int32), part, part, small, part, part, small, part, part, part, part,
+            *rows, pltpu.SMEM((RAND,) + random_blocks.shape[:2], jnp.int32), pltpu.VMEM((1, global_positions.shape[0]), jnp.int32), part, part, small, part, part, small, part, part, part, part,
             pltpu.VMEM((total, 128), bf16),
             pltpu.VMEM((total, 128), bf16),
             pltpu.VMEM((n, total, tokens), f32),
             pltpu.VMEM((n, total, tokens), bf16),
             pltpu.VMEM((n, total, tokens), bf16),
             pltpu.SemaphoreType.DMA((6,)),
-            pltpu.SemaphoreType.DMA((4,)),
             pltpu.SemaphoreType.DMA((5, n - 1)),
             pltpu.SemaphoreType.DMA((5, n - 1)),
         ],
@@ -579,11 +561,10 @@
     return pl.pallas_call(
         write_out,
         out_shape=[jax.ShapeDtypeStruct((tokens, width), bf16)] * 4,
-        in_specs=[where_it_lies] * 4,
+        in_specs=[pl.BlockSpec(memory_space=pltpu.VMEM)] * 4,
         out_specs=[where_it_lies] * 4,
-        scratch_shapes=rows + [pltpu.SemaphoreType.DMA((2, 4))],
-        compiler_params=pltpu.CompilerParams(vmem_limit_bytes=LIMIT),
-    )(*results)
+        scratch_shapes=[pltpu.SemaphoreType.DMA((4,))],
+    )(*(pltpu.with_memory_space_constraint(r, pltpu.VMEM) for r in results))
 
 
 def local(query_rows, key_rows, value_rows, out_grad, random_blocks, global_positions):

time: 33 us -> 31.3 us (0.948)
  Pallas kernels: 32.2 us -> 30.5 us
    pallas_call x1, Pallas kernels: 1.82 us -> 0.82 us  [local_heads(): pl.pallas_call(write_out, out_shape=[jax.ShapeDtypeStruct((tokens, width)...]
    pallas_call x1, Pallas kernels: 30.4 us -> 29.7 us  [local_heads(): pl.pallas_call(partial(head_kernel, n, tokens), out_shape=[pltpu.VMEM((to...]
where the time goes in v1:
time: 31.3 us; the launch traced here: 31.2 us
  Pallas kernels  30.5 us (97%)
  between operations  0.64 us (2%)
    pallas_call x1, Pallas kernels, local_heads(): pl.pallas_call(partial(head_kernel, n, tokens), out_shape=[pltpu.VMEM((to...  29.7 us
    pallas_call x1, Pallas kernels, local_heads(): pl.pallas_call(write_out, out_shape=[jax.ShapeDtypeStruct((tokens, width)...  0.82 us

profile of v1, /device:TPU:0, one launch (start us, length us, event | category | flops | bytes accessed | tf_op | source)
XLA Modules:
  0.0 31.2 jit_solution(6708288947930793715)
XLA Ops:
  0.6 29.7 %shard_map.93 = (bf16[256,256]{1,0:T(8,128)(2,1)S(1)}, bf16[256,256]{1,0:T(8,128)(2,1)S(1)}, bf16[256,256]{1,0:T(8,128)(2,1)S(1)}, bf16[256,256]{1,0:T(8,128)(2,1)S(1)}) custom-call(bf16[256,256]{1,0:T(8,128)(2,1)} %q_hbm.1, bf16[256,256]{1,0:T(8,128)(2,1)} %k_hbm.1, bf16[256,256]{1,0:T(8,128)(2,1)} %v_hbm.1, bf16[256,256]{1,0:T(8,128)(2,1)} %g_hbm.1, ...), custom_call_target="tpu_custom_call" | custom-call | flops 939524096 | bytes 1048576 | tf_op jit(solution)/shard_map/pallas_call | solution.py:535
  30.4 0.8 %shard_map.94 = (bf16[256,256]{1,0:T(8,128)(2,1)}, bf16[256,256]{1,0:T(8,128)(2,1)}, bf16[256,256]{1,0:T(8,128)(2,1)}, bf16[256,256]{1,0:T(8,128)(2,1)}) custom-call(bf16[256,256]{1,0:T(8,128)(2,1)S(1)} %get-tuple-element.8.refs_0_, bf16[256,256]{1,0:T(8,128)(2,1)S(1)} %get-tuple-element.9.refs_1_, bf16[256,256]{1,0:T(8,128)(2,1)S(1)} %get-tuple-element.10.refs_2_, ...), custom_call_target="tpu_custom_call" | custom-call | tf_op jit(solution)/shard_map/pallas_call | solution.py:561

commit v2 on v1

--- a/solution.py
+++ b/solution.py
@@ -329,56 +329,81 @@
 
 def head_kernel(
     n, tokens, q_hbm, k_hbm, v_hbm, g_hbm, rb_hbm, gp_hbm, att_ref, dq_ref, dk_ref, dv_ref,
-    q_ref, k_ref, v_ref, g_ref, rb_ref, gp_ref, kq_send, vd_send, tab_send, kq, vd, tab, o1_send, o2_send, o1, o2,
-    ka, qa, probs, weights, dscore, load_sem, send_sem, recv_sem,
+    q_ref, k_ref, v_ref, g_ref, rb_ref, gp_ref, kq_send, v_send, g_send, tab_send, kq, vp, gp, tab,
+    att_send, dv_send, dq_send, dk_send, att, dv, dq, dk,
+    ka, qa, va, ga, probs, weights, dscore, load_sem, turn, send_sem, recv_sem,
 ):
     me = lax.axis_index("seq")
     total = n * tokens
+    part = tokens // 2
     qb = tokens // BLK
     scale = 1.0 / math.sqrt(HD)
-    peers = [lax.rem(me + off, n) for off in range(1, n)]
-    sources = [lax.rem(me + n - off, n) for off in range(1, n)]
-
+    half = me // 2
+    inner = (me % 3 + 1) // 2
+    near, far, mate = 2 - 2 * half, 3 - 2 * half, 1 - me + 4 * half
+    others = [
+        inner * mate + (1 - inner) * near,
+        inner * near + (1 - inner) * far,
+        inner * far + (1 - inner) * mate,
+    ]
+
+    barrier = pltpu.get_barrier_semaphore()
+    for peer in others:
+        pl.semaphore_signal(
+            barrier, inc=1, device_id={"seq": peer}, device_id_type=pl.DeviceIdType.MESH
+        )
     loads = [
         pltpu.make_async_copy(hbm, vmem, load_sem.at[i])
         for i, (hbm, vmem) in enumerate(
             ((k_hbm, k_ref), (q_hbm, q_ref), (v_hbm, v_ref), (g_hbm, g_ref), (rb_hbm, rb_ref), (gp_hbm, gp_ref))
         )
     ]
-    for load in loads:
-        load.start()
-    barrier = pltpu.get_barrier_semaphore()
-    for peer in peers:
-        pl.semaphore_signal(
-            barrier, inc=1, device_id={"seq": peer}, device_id_type=pl.DeviceIdType.MESH
-        )
-
-    def copy(stage, off, send, recv, slot):
+    for i in (4, 0, 1, 2, 3, 5):
+        loads[i].start()
+
+    stages = (
+        (tab_send, tab), (kq_send, kq), (v_send, vp), (g_send, gp),
+        (att_send, att), (dv_send, dv), (dq_send, dq), (dk_send, dk),
+    )
+
+    def copy(stage, peer, slot):
+        send, recv = stages[stage]
         return pltpu.make_async_remote_copy(
-            src_ref=send.at[peers[off - 1]],
+            src_ref=send.at[peer],
             dst_ref=recv.at[slot],
-            send_sem=send_sem.at[stage, off - 1],
-            recv_sem=recv_sem.at[stage, off - 1],
-            device_id={"seq": peers[off - 1]},
+            send_sem=send_sem.at[stage, peer],
+            recv_sem=recv_sem.at[stage, slot],
+            device_id={"seq": peer},
             device_id_type=pl.DeviceIdType.MESH,
         )
 
-    def start(stage, off, send, recv):
-        copy(stage, off, send, recv, me).start()
-
-    def arrive(stage, off, send, recv):
-        copy(stage, off, send, recv, sources[off - 1]).wait_recv()
-
-    row = lax.broadcasted_iota(jnp.int32, (8, 128), 0)
-    lane = lax.broadcasted_iota(jnp.int32, (8, 128), 1)
+    def start(stage, peer):
+        copy(stage, peer, me).start()
+
+    def arrive(stage):
+        for peer in others:
+            copy(stage, peer, peer).wait_recv()
+
+    def keep(stage):
+        send, recv = stages[stage]
+        recv[me] = send[me]
+
+    def fold(ref, slot, rows):
+        ref[slot, :, 0:HD] = rows[0:part]
+        ref[slot, :, HD : 2 * HD] = rows[part:tokens]
+
+    def fold_t(ref, slot, columns):
+        stacked = jnp.concatenate([columns[:, 0:part], columns[:, part:tokens]], axis=0)
+        ref[slot] = stacked.T.astype(jnp.bfloat16)
+
+    lane = lax.broadcasted_iota(jnp.int32, (1, 128), 1)
     loads[4].wait()
     for h in range(n):
-        mark = jnp.zeros((8, 128), jnp.float32)
-        for b in range(qb):
-            hit = lane == rb_ref[0, h, b]
-            for r in range(1, RAND):
-                hit = hit | (lane == rb_ref[r, h, b])
-            mark = jnp.where(hit & (row == b), 1.0, mark)
+        mark = jnp.zeros((1, 128), jnp.int32)
+        for r in range(RAND):
+            for b in range(qb):
+                at = lax.rem(HD + r * 8 * n + 8 * me + b, 128)
+                mark = jnp.where(lane == at, rb_ref[r, h, b], mark)
         tab_send[h] = mark
     loads[0].wait()
     loads[1].wait()
@@ -387,21 +412,31 @@
         kq_send[h, :, 0:HD] = k_ref[:, cols]
         kq_send[h, :, HD : 2 * HD] = q_ref[:, cols] * jnp.bfloat16(scale)
     pl.semaphore_wait(barrier, n - 1)
-    order = [2, 1, 3] if n == 4 else list(range(1, n))
-    for off in order:
-        start(0, off, tab_send, tab)
-        start(1, off, kq_send, kq)
+    for peer in others:
+        start(0, peer)
+        start(1, peer)
     loads[2].wait()
+    for h in range(n):
+        fold(v_send, h, v_ref[:, h * HD : (h + 1) * HD])
     loads[3].wait()
     for h in range(n):
-        cols = slice(h * HD, (h + 1) * HD)
-        vd_send[h, :, 0:HD] = v_ref[:, cols]
-        vd_send[h, :, HD : 2 * HD] = g_ref[:, cols]
-    for off in order:
-        start(2, off, vd_send, vd)
-    kq[me] = kq_send[me]
-    vd[me] = vd_send[me]
-    tab[me] = tab_send[me]
+        fold(g_send, h, g_ref[:, h * HD : (h + 1) * HD])
+
+    def take_turns(stage):
+        copy(stage, near, me).wait_send()
+
+        @pl.when(inner == 1)
+        def _():
+            pl.semaphore_signal(
+                turn.at[stage - 1], inc=1, device_id={"seq": mate}, device_id_type=pl.DeviceIdType.MESH
+            )
+
+        @pl.when(inner == 0)
+        def _():
+            pl.semaphore_wait(turn.at[stage - 1], 1)
+
+        for peer in others:
+            start(stage + 1, peer)
 
     pos = lax.broadcasted_iota(jnp.int32, (total, 128), 0)
     col = lax.broadcasted_iota(jnp.int32, (total, 128), 1)
@@ -418,24 +453,23 @@
     block = (slot // 8) * qb + slot % 8
     mine = (slot >= 0) & (slot < 8 * n) & (slot % 8 < qb)
     key_block = pos // BLK
-    near = mine & (block - key_block <= 1) & (key_block - block <= 1)
-    open_key = near | is_global
+    window = mine & (block - key_block <= 1) & (key_block - block <= 1)
+    open_key = window | is_global
     hot = jnp.where(mine & (block == key_block) & jnp.logical_not(is_global), 1.0, 0.0)
-    place = jnp.where(col == key_block, 1.0, 0.0).astype(jnp.bfloat16)
-
-    for off in order:
-        arrive(0, off, tab_send, tab)
-        arrive(1, off, kq_send, kq)
-    table = jnp.concatenate(
-        [
-            jnp.zeros((HD, 128), jnp.float32),
-            tab[...].reshape(8 * n, 128),
-            jnp.zeros((128 - HD - 8 * n, 128), jnp.float32),
-        ],
-        axis=0,
-    ).astype(jnp.bfloat16)
-    chosen = mm(place, table, NT)
-    bias = jnp.where(open_key | (chosen > 0.5), 0.0, -BIG).astype(jnp.bfloat16)
+
+    take_turns(1)
+    for stage in range(4):
+        keep(stage)
+
+    arrive(0)
+    picks = tab[0]
+    for c in range(1, n):
+        picks = picks + tab[c]
+    for r in range(RAND):
+        shifted = picks if r == 0 else pltpu.roll(picks, 128 - r * 8 * n, 1)
+        open_key = open_key | (mine & (key_block == shifted))
+    bias = jnp.where(open_key, 0.0, -BIG).astype(jnp.bfloat16)
+    arrive(1)
     pair = kq[...].reshape(total, 128)
     ka[...] = bias
     ka[:, 0:HD] = pair[:, 0:HD]
@@ -444,73 +478,96 @@
 
     keys = ka[...]
     for a in range(n):
-        rows = pl.ds(a * tokens, tokens)
-        score = mm(keys, qa[rows, :], NT)
+        score = mm(keys, qa[a * tokens : (a + 1) * tokens, :], NT)
         top = jnp.max(score, axis=0, keepdims=True)
         raised = jnp.exp(score - top)
         prob = raised * (1.0 / jnp.sum(raised, axis=0, keepdims=True))
         probs[a] = prob
         weights[a] = prob.astype(jnp.bfloat16)
-
-    for off in order:
-        arrive(2, off, vd_send, vd)
-    values = vd[...].reshape(total, 2 * HD)[:, 0:HD]
+    keys_t = keys[:, 0:HD].T
+    take_turns(2)
+
+    order = others + [me]
+    arrive(2)
+    for c in range(n):
+        va[c * tokens : c * tokens + part, :] = vp[c, :, 0:HD]
+        va[c * tokens + part : (c + 1) * tokens, :] = vp[c, :, HD : 2 * HD]
+    values = va[...]
     values_t = values.T
-    keys_t = keys[:, 0:HD].T
-    steps = order + [0]
-    deltas = []
-    for off in steps:
-        a = lax.rem(me + off, n)
+    outs = []
+    for a in order:
+        out = mm(values_t, weights[a], NN)
+        fold_t(att_send, a, out)
+        if a is not me:
+            start(4, a)
+        outs.append(out.astype(jnp.bfloat16).astype(jnp.float32))
+
+    arrive(3)
+    for c in range(n):
+        ga[c, 0:part, :] = gp[c, :, 0:HD]
+        ga[c, part:tokens, :] = gp[c, :, HD : 2 * HD]
+
+    def value_grad(a):
         rows = pl.ds(pl.multiple_of(a * tokens, tokens), tokens)
-        out = mm(values_t, weights[a], NN).T.astype(jnp.bfloat16)
-        grad = vd[a, :, HD : 2 * HD]
-        deltas.append(jnp.sum(grad.astype(jnp.float32).T * out.astype(jnp.float32).T, axis=0, keepdims=True))
-        dv = jnp.zeros((tokens, HD), jnp.float32)
+        grad = jnp.zeros((tokens, HD), jnp.float32)
         for c in range(n):
-            dv = dv + mm(weights[c, rows, :], vd[c, :, HD : 2 * HD], NN)
-        o1_send[a, :, 0:HD] = out
-        o1_send[a, :, HD : 2 * HD] = dv.astype(jnp.bfloat16)
-        if off:
-            start(3, off, o1_send, o1)
-        else:
-            o1[me] = o1_send[me]
-
-    for step, off in enumerate(steps):
-        a = lax.rem(me + off, n)
-        dprob = mm(values, vd[a, :, HD : 2 * HD], NT)
-        ds = (probs[a] * (dprob - deltas[step])).astype(jnp.bfloat16)
-        dscore[a] = ds
-        dq = mm(keys_t, ds, NN).T * scale
-        o2_send[a, :, 0:HD] = dq.astype(jnp.bfloat16)
-    for off in steps:
-        a = lax.rem(me + off, n)
+            grad = grad + mm(weights[c, rows, :], ga[c], NN)
+        fold(dv_send, a, grad.astype(jnp.bfloat16))
+
+    def score_grad(a, out):
+        grad = ga[a]
+        delta = jnp.sum(grad.astype(jnp.float32).T * out, axis=0, keepdims=True)
+        dprob = mm(values, grad, NT)
+        dscore[a] = (probs[a] * (dprob - delta)).astype(jnp.bfloat16)
+
+    def query_grad(a):
+        fold_t(dq_send, a, mm(keys_t, dscore[a], NN) * scale)
+
+    def key_grad(a):
         rows = pl.ds(pl.multiple_of(a * tokens, tokens), tokens)
-        dk = jnp.zeros((tokens, HD), jnp.float32)
+        grad = jnp.zeros((tokens, HD), jnp.float32)
         for c in range(n):
-            dk = dk + mm(dscore[c, rows, :], qa[c * tokens : (c + 1) * tokens, 0:HD], NN)
-        o2_send[a, :, HD : 2 * HD] = dk.astype(jnp.bfloat16)
-        if off:
-            start(4, off, o2_send, o2)
-        else:
-            o2[me] = o2_send[me]
-
-    for off in order:
-        arrive(3, off, o1_send, o1)
-    for h in range(n):
-        cols = slice(h * HD, (h + 1) * HD)
-        att_ref[:, cols] = o1[h, :, 0:HD]
-        dv_ref[:, cols] = o1[h, :, HD : 2 * HD]
-    for off in order:
-        arrive(4, off, o2_send, o2)
-    for h in range(n):
-        cols = slice(h * HD, (h + 1) * HD)
-        dq_ref[:, cols] = o2[h, :, 0:HD]
-        dk_ref[:, cols] = o2[h, :, HD : 2 * HD]
-    for stage, (send, recv) in enumerate(
-        ((tab_send, tab), (kq_send, kq), (vd_send, vd), (o1_send, o1), (o2_send, o2))
-    ):
-        for off in order:
-            copy(stage, off, send, recv, me).wait_send()
+            grad = grad + mm(dscore[c, rows, :], qa[c * tokens : (c + 1) * tokens, 0:HD], NN)
+        fold(dk_send, a, grad.astype(jnp.bfloat16))
+
+    value_grad(order[0])
+    start(5, order[0])
+    value_grad(order[1])
+    start(5, order[1])
+    value_grad(order[2])
+    start(5, order[2])
+    score_grad(order[0], outs[0])
+    query_grad(order[0])
+    start(6, order[0])
+    score_grad(order[1], outs[1])
+    score_grad(order[2], outs[2])
+    score_grad(order[3], outs[3])
+    key_grad(order[0])
+    start(7, order[0])
+    query_grad(order[1])
+    start(6, order[1])
+    key_grad(order[1])
+    start(7, order[1])
+    query_grad(order[2])
+    start(6, order[2])
+    key_grad(order[2])
+    start(7, order[2])
+    value_grad(order[3])
+    query_grad(order[3])
+    key_grad(order[3])
+    for stage in range(4, 8):
+        keep(stage)
+
+    for stage, ref in ((4, att_ref), (5, dv_ref), (6, dq_ref), (7, dk_ref)):
+        arrive(stage)
+        recv = stages[stage][1]
+        for h in range(n):
+            cols = slice(h * HD, (h + 1) * HD)
+            ref[0:part, cols] = recv[h, :, 0:HD]
+            ref[part:tokens, cols] = recv[h, :, HD : 2 * HD]
+    for stage in range(len(stages)):
+        for peer in (far, mate) if stage in (1, 2) else others:
+            copy(stage, peer, me).wait_send()
 
 
 def write_out(*refs):
@@ -530,23 +587,32 @@
     bf16, f32 = jnp.bfloat16, jnp.float32
     where_it_lies = pl.BlockSpec(memory_space=pltpu.HBM)
     rows = [pltpu.VMEM((tokens, width), bf16)] * 4
-    part = pltpu.VMEM((n, tokens, 2 * HD), bf16)
-    small = pltpu.VMEM((n, 8, 128), f32)
+    whole = pltpu.VMEM((n, tokens, 2 * HD), bf16)
+    folded = pltpu.VMEM((n, tokens // 2, 2 * HD), bf16)
+    small = pltpu.VMEM((n, 1, 128), jnp.int32)
     results = pl.pallas_call(
         partial(head_kernel, n, tokens),
         out_shape=[pltpu.VMEM((tokens, width), bf16)] * 4,
         in_specs=[where_it_lies] * 6,
         out_specs=[pl.BlockSpec(memory_space=pltpu.VMEM)] * 4,
         scratch_shapes=[
-            *rows, pltpu.SMEM((RAND,) + random_blocks.shape[:2], jnp.int32), pltpu.VMEM((1, global_positions.shape[0]), jnp.int32), part, part, small, part, part, small, part, part, part, part,
+            *rows,
+            pltpu.SMEM((RAND,) + random_blocks.shape[:2], jnp.int32),
+            pltpu.VMEM((1, global_positions.shape[0]), jnp.int32),
+            whole, folded, folded, small,
+            whole, folded, folded, small,
+            *([folded] * 8),
             pltpu.VMEM((total, 128), bf16),
             pltpu.VMEM((total, 128), bf16),
+            pltpu.VMEM((total, HD), bf16),
+            pltpu.VMEM((n, tokens, HD), bf16),
             pltpu.VMEM((n, total, tokens), f32),
             pltpu.VMEM((n, total, tokens), bf16),
             pltpu.VMEM((n, total, tokens), bf16),
             pltpu.SemaphoreType.DMA((6,)),
-            pltpu.SemaphoreType.DMA((5, n - 1)),
-            pltpu.SemaphoreType.DMA((5, n - 1)),
+            pltpu.SemaphoreType.REGULAR((2,)),
+            pltpu.SemaphoreType.DMA((8, n)),
+            pltpu.SemaphoreType.DMA((8, n)),
         ],
         compiler_params=pltpu.CompilerParams(
             collective_id=0, has_side_effects=True, vmem_limit_bytes=LIMIT
@@ -571,7 +637,7 @@
     n = lax.axis_size("seq")
     tokens = query_rows.shape[0]
     one_head_each = query_rows.shape[1] == n * HD and n > 1
-    fits = 8 * n <= 128 - HD and tokens // BLK <= 8 and n * tokens // BLK <= 128
+    fits = n == 4 and 8 * n <= 128 - HD and tokens // BLK <= 8 and n * tokens // BLK <= 128
     if one_head_each and fits and tokens % 256 == 0 and n * tokens <= 1024:
         run = local_heads
     else:

time: 31.3 us -> 31 us (level)
    pallas_call x1, Pallas kernels: 29.7 us -> 29.4 us  [local_heads(): pl.pallas_call(partial(head_kernel, n, tokens), out_shape=[pltpu.VMEM((to...]
where the time goes in v2:
time: 31 us; the launch traced here: 30.8 us
  Pallas kernels  30.2 us (97%)
  between operations  0.64 us (2%)
    pallas_call x1, Pallas kernels, local_heads(): pl.pallas_call(partial(head_kernel, n, tokens), out_shape=[pltpu.VMEM((to...  29.4 us
    pallas_call x1, Pallas kernels, local_heads(): pl.pallas_call(write_out, out_shape=[jax.ShapeDtypeStruct((tokens, width)...  0.82 us

profile of v2, /device:TPU:0, one launch (start us, length us, event | category | flops | bytes accessed | tf_op | source)
XLA Modules:
  0.0 30.8 jit_solution(11207154739954225359)
XLA Ops:
  0.6 29.4 %shard_map.93 = (bf16[256,256]{1,0:T(8,128)(2,1)S(1)}, bf16[256,256]{1,0:T(8,128)(2,1)S(1)}, bf16[256,256]{1,0:T(8,128)(2,1)S(1)}, bf16[256,256]{1,0:T(8,128)(2,1)S(1)}) custom-call(bf16[256,256]{1,0:T(8,128)(2,1)} %q_hbm.1, bf16[256,256]{1,0:T(8,128)(2,1)} %k_hbm.1, bf16[256,256]{1,0:T(8,128)(2,1)} %v_hbm.1, bf16[256,256]{1,0:T(8,128)(2,1)} %g_hbm.1, ...), custom_call_target="tpu_custom_call" | custom-call | flops 939524096 | bytes 1048576 | tf_op jit(solution)/shard_map/pallas_call | solution.py:593
  30.0 0.8 %shard_map.94 = (bf16[256,256]{1,0:T(8,128)(2,1)}, bf16[256,256]{1,0:T(8,128)(2,1)}, bf16[256,256]{1,0:T(8,128)(2,1)}, bf16[256,256]{1,0:T(8,128)(2,1)}) custom-call(bf16[256,256]{1,0:T(8,128)(2,1)S(1)} %get-tuple-element.8.refs_0_, bf16[256,256]{1,0:T(8,128)(2,1)S(1)} %get-tuple-element.9.refs_1_, bf16[256,256]{1,0:T(8,128)(2,1)S(1)} %get-tuple-element.10.refs_2_, ...), custom_call_target="tpu_custom_call" | custom-call | tf_op jit(solution)/shard_map/pallas_call | solution.py:627

commit v3 on v2

--- a/solution.py
+++ b/solution.py
@@ -412,9 +412,12 @@
         kq_send[h, :, 0:HD] = k_ref[:, cols]
         kq_send[h, :, HD : 2 * HD] = q_ref[:, cols] * jnp.bfloat16(scale)
     pl.semaphore_wait(barrier, n - 1)
-    for peer in others:
-        start(0, peer)
-        start(1, peer)
+    @pl.when(inner == 1)
+    def _():
+        for peer in others:
+            start(0, peer)
+            start(1, peer)
+
     loads[2].wait()
     for h in range(n):
         fold(v_send, h, v_ref[:, h * HD : (h + 1) * HD])
@@ -422,21 +425,13 @@
     for h in range(n):
         fold(g_send, h, g_ref[:, h * HD : (h + 1) * HD])
 
-    def take_turns(stage):
-        copy(stage, near, me).wait_send()
-
-        @pl.when(inner == 1)
-        def _():
-            pl.semaphore_signal(
-                turn.at[stage - 1], inc=1, device_id={"seq": mate}, device_id_type=pl.DeviceIdType.MESH
-            )
-
-        @pl.when(inner == 0)
-        def _():
-            pl.semaphore_wait(turn.at[stage - 1], 1)
-
-        for peer in others:
-            start(stage + 1, peer)
+    @pl.when(inner == 1)
+    def _():
+        for stage in (2, 3):
+            for peer in others:
+                start(stage, peer)
+        copy(1, mate, me).wait_send()
+        pl.semaphore_signal(turn, inc=1, device_id={"seq": mate}, device_id_type=pl.DeviceIdType.MESH)
 
     pos = lax.broadcasted_iota(jnp.int32, (total, 128), 0)
     col = lax.broadcasted_iota(jnp.int32, (total, 128), 1)
@@ -457,9 +452,21 @@
     open_key = window | is_global
     hot = jnp.where(mine & (block == key_block) & jnp.logical_not(is_global), 1.0, 0.0)
 
-    take_turns(1)
+    @pl.when(inner == 0)
+    def _():
+        pl.semaphore_wait(turn, 1)
+        for stage in (0, 1, 2):
+            for peer in others:
+                start(stage, peer)
+
     for stage in range(4):
         keep(stage)
+
+    @pl.when(inner == 0)
+    def _():
+        copy(2, far, me).wait_send()
+        for peer in others:
+            start(3, peer)
 
     arrive(0)
     picks = tab[0]
@@ -485,7 +492,6 @@
         probs[a] = prob
         weights[a] = prob.astype(jnp.bfloat16)
     keys_t = keys[:, 0:HD].T
-    take_turns(2)
 
     order = others + [me]
     arrive(2)
@@ -534,8 +540,6 @@
     start(5, order[0])
     value_grad(order[1])
     start(5, order[1])
-    value_grad(order[2])
-    start(5, order[2])
     score_grad(order[0], outs[0])
     query_grad(order[0])
     start(6, order[0])
@@ -548,6 +552,8 @@
     start(6, order[1])
     key_grad(order[1])
     start(7, order[1])
+    value_grad(order[2])
+    start(5, order[2])
     query_grad(order[2])
     start(6, order[2])
     key_grad(order[2])
@@ -565,8 +571,16 @@
             cols = slice(h * HD, (h + 1) * HD)
             ref[0:part, cols] = recv[h, :, 0:HD]
             ref[part:tokens, cols] = recv[h, :, HD : 2 * HD]
+    @pl.when(inner == 1)
+    def _():
+        copy(2, far, me).wait_send()
+
+    @pl.when(inner == 0)
+    def _():
+        copy(1, mate, me).wait_send()
+
     for stage in range(len(stages)):
-        for peer in (far, mate) if stage in (1, 2) else others:
+        for peer in (near, far) if stage == 1 else (mate, near) if stage == 2 else others:
             copy(stage, peer, me).wait_send()
 
 
@@ -610,7 +624,7 @@
             pltpu.VMEM((n, total, tokens), bf16),
             pltpu.VMEM((n, total, tokens), bf16),
             pltpu.SemaphoreType.DMA((6,)),
-            pltpu.SemaphoreType.REGULAR((2,)),
+            pltpu.SemaphoreType.REGULAR,
             pltpu.SemaphoreType.DMA((8, n)),
             pltpu.SemaphoreType.DMA((8, n)),
         ],

time: 31 us -> 29.7 us (0.958)
  Pallas kernels: 30.2 us -> 28.8 us
    pallas_call x1, Pallas kernels: 29.4 us -> 28 us  [local_heads(): pl.pallas_call(partial(head_kernel, n, tokens), out_shape=[pltpu.VMEM((to...]
where the time goes in v3:
time: 29.7 us; the launch traced here: 29.5 us
  Pallas kernels  28.8 us (97%)
  between operations  0.64 us (2%)
    pallas_call x1, Pallas kernels, local_heads(): pl.pallas_call(partial(head_kernel, n, tokens), out_shape=[pltpu.VMEM((to...  28 us
    pallas_call x1, Pallas kernels, local_heads(): pl.pallas_call(write_out, out_shape=[jax.ShapeDtypeStruct((tokens, width)...  0.82 us

profile of v3, /device:TPU:0, one launch (start us, length us, event | category | flops | bytes accessed | tf_op | source)
XLA Modules:
  0.0 29.5 jit_solution(16868914693814857148)
XLA Ops:
  0.6 28.0 %shard_map.93 = (bf16[256,256]{1,0:T(8,128)(2,1)S(1)}, bf16[256,256]{1,0:T(8,128)(2,1)S(1)}, bf16[256,256]{1,0:T(8,128)(2,1)S(1)}, bf16[256,256]{1,0:T(8,128)(2,1)S(1)}) custom-call(bf16[256,256]{1,0:T(8,128)(2,1)} %q_hbm.1, bf16[256,256]{1,0:T(8,128)(2,1)} %k_hbm.1, bf16[256,256]{1,0:T(8,128)(2,1)} %v_hbm.1, bf16[256,256]{1,0:T(8,128)(2,1)} %g_hbm.1, ...), custom_call_target="tpu_custom_call" | custom-call | flops 939524096 | bytes 1048576 | tf_op jit(solution)/shard_map/pallas_call | solution.py:607
  28.7 0.8 %shard_map.94 = (bf16[256,256]{1,0:T(8,128)(2,1)}, bf16[256,256]{1,0:T(8,128)(2,1)}, bf16[256,256]{1,0:T(8,128)(2,1)}, bf16[256,256]{1,0:T(8,128)(2,1)}) custom-call(bf16[256,256]{1,0:T(8,128)(2,1)S(1)} %get-tuple-element.8.refs_0_, bf16[256,256]{1,0:T(8,128)(2,1)S(1)} %get-tuple-element.9.refs_1_, bf16[256,256]{1,0:T(8,128)(2,1)S(1)} %get-tuple-element.10.refs_2_, ...), custom_call_target="tpu_custom_call" | custom-call | tf_op jit(solution)/shard_map/pallas_call | solution.py:641

commit v4 on v3

--- a/solution.py
+++ b/solution.py
@@ -504,7 +504,7 @@
     for a in order:
         out = mm(values_t, weights[a], NN)
         fold_t(att_send, a, out)
-        if a is not me:
+        if a is not me and a is not others[2]:
             start(4, a)
         outs.append(out.astype(jnp.bfloat16).astype(jnp.float32))
 
@@ -552,6 +552,7 @@
     start(6, order[1])
     key_grad(order[1])
     start(7, order[1])
+    start(4, order[2])
     value_grad(order[2])
     start(5, order[2])
     query_grad(order[2])

time: 29.7 us -> 29.3 us (0.987)
  Pallas kernels: 28.8 us -> 28.4 us
    pallas_call x1, Pallas kernels: 28 us -> 27.6 us  [local_heads(): pl.pallas_call(partial(head_kernel, n, tokens), out_shape=[pltpu.VMEM((to...]
where the time goes in v4:
time: 29.3 us; the launch traced here: 29.1 us
  Pallas kernels  28.4 us (97%)
  between operations  0.64 us (2%)
    pallas_call x1, Pallas kernels, local_heads(): pl.pallas_call(partial(head_kernel, n, tokens), out_shape=[pltpu.VMEM((to...  27.6 us
    pallas_call x1, Pallas kernels, local_heads(): pl.pallas_call(write_out, out_shape=[jax.ShapeDtypeStruct((tokens, width)...  0.82 us

profile of v4, /device:TPU:0, one launch (start us, length us, event | category | flops | bytes accessed | tf_op | source)
XLA Modules:
  0.0 29.1 jit_solution(12145163346289144848)
XLA Ops:
  0.6 27.6 %shard_map.93 = (bf16[256,256]{1,0:T(8,128)(2,1)S(1)}, bf16[256,256]{1,0:T(8,128)(2,1)S(1)}, bf16[256,256]{1,0:T(8,128)(2,1)S(1)}, bf16[256,256]{1,0:T(8,128)(2,1)S(1)}) custom-call(bf16[256,256]{1,0:T(8,128)(2,1)} %q_hbm.1, bf16[256,256]{1,0:T(8,128)(2,1)} %k_hbm.1, bf16[256,256]{1,0:T(8,128)(2,1)} %v_hbm.1, bf16[256,256]{1,0:T(8,128)(2,1)} %g_hbm.1, ...), custom_call_target="tpu_custom_call" | custom-call | flops 939524096 | bytes 1048576 | tf_op jit(solution)/shard_map/pallas_call | solution.py:608
  28.2 0.8 %shard_map.94 = (bf16[256,256]{1,0:T(8,128)(2,1)}, bf16[256,256]{1,0:T(8,128)(2,1)}, bf16[256,256]{1,0:T(8,128)(2,1)}, bf16[256,256]{1,0:T(8,128)(2,1)}) custom-call(bf16[256,256]{1,0:T(8,128)(2,1)S(1)} %get-tuple-element.8.refs_0_, bf16[256,256]{1,0:T(8,128)(2,1)S(1)} %get-tuple-element.9.refs_1_, bf16[256,256]{1,0:T(8,128)(2,1)S(1)} %get-tuple-element.10.refs_2_, ...), custom_call_target="tpu_custom_call" | custom-call | tf_op jit(solution)/shard_map/pallas_call | solution.py:642

commit v5 on v4

--- a/solution.py
+++ b/solution.py
@@ -414,7 +414,7 @@
     pl.semaphore_wait(barrier, n - 1)
     @pl.when(inner == 1)
     def _():
-        for peer in others:
+        for peer in (near, far, mate):
             start(0, peer)
             start(1, peer)
 
@@ -565,13 +565,20 @@
     for stage in range(4, 8):
         keep(stage)
 
-    for stage, ref in ((4, att_ref), (5, dv_ref), (6, dq_ref), (7, dk_ref)):
-        arrive(stage)
+    def unpack(stage, ref):
         recv = stages[stage][1]
         for h in range(n):
+
+            @pl.when(me != h)
+            def _():
+                copy(stage, h, h).wait_recv()
+
             cols = slice(h * HD, (h + 1) * HD)
             ref[0:part, cols] = recv[h, :, 0:HD]
             ref[part:tokens, cols] = recv[h, :, HD : 2 * HD]
+
+    for stage, ref in ((4, att_ref), (5, dv_ref), (6, dq_ref)):
+        unpack(stage, ref)
     @pl.when(inner == 1)
     def _():
         copy(2, far, me).wait_send()
@@ -580,9 +587,12 @@
     def _():
         copy(1, mate, me).wait_send()
 
-    for stage in range(len(stages)):
+    for stage in range(7):
         for peer in (near, far) if stage == 1 else (mate, near) if stage == 2 else others:
             copy(stage, peer, me).wait_send()
+    unpack(7, dk_ref)
+    for peer in others:
+        copy(7, peer, me).wait_send()
 
 
 def write_out(*refs):

time: 29.3 us -> 29.2 us (level)
  no operation moved by 1% of the time
where the time goes in v5:
time: 29.2 us; the launch traced here: 29 us
  Pallas kernels  28.4 us (97%)
  between operations  0.64 us (2%)
    pallas_call x1, Pallas kernels, local_heads(): pl.pallas_call(partial(head_kernel, n, tokens), out_shape=[pltpu.VMEM((to...  27.5 us
    pallas_call x1, Pallas kernels, local_heads(): pl.pallas_call(write_out, out_shape=[jax.ShapeDtypeStruct((tokens, width)...  0.82 us

profile of v5, /device:TPU:0, one launch (start us, length us, event | category | flops | bytes accessed | tf_op | source)
XLA Modules:
  0.0 29.0 jit_solution(4375787002539536881)
XLA Ops:
  0.6 27.5 %shard_map.93 = (bf16[256,256]{1,0:T(8,128)(2,1)S(1)}, bf16[256,256]{1,0:T(8,128)(2,1)S(1)}, bf16[256,256]{1,0:T(8,128)(2,1)S(1)}, bf16[256,256]{1,0:T(8,128)(2,1)S(1)}) custom-call(bf16[256,256]{1,0:T(8,128)(2,1)} %q_hbm.1, bf16[256,256]{1,0:T(8,128)(2,1)} %k_hbm.1, bf16[256,256]{1,0:T(8,128)(2,1)} %v_hbm.1, bf16[256,256]{1,0:T(8,128)(2,1)} %g_hbm.1, ...), custom_call_target="tpu_custom_call" | custom-call | flops 939524096 | bytes 1048576 | tf_op jit(solution)/shard_map/pallas_call | solution.py:618
  28.2 0.8 %shard_map.94 = (bf16[256,256]{1,0:T(8,128)(2,1)}, bf16[256,256]{1,0:T(8,128)(2,1)}, bf16[256,256]{1,0:T(8,128)(2,1)}, bf16[256,256]{1,0:T(8,128)(2,1)}) custom-call(bf16[256,256]{1,0:T(8,128)(2,1)S(1)} %get-tuple-element.8.refs_0_, bf16[256,256]{1,0:T(8,128)(2,1)S(1)} %get-tuple-element.9.refs_1_, bf16[256,256]{1,0:T(8,128)(2,1)S(1)} %get-tuple-element.10.refs_2_, ...), custom_call_target="tpu_custom_call" | custom-call | tf_op jit(solution)/shard_map/pallas_call | solution.py:652
